TPU v7x, 32 devices: a whole 2x2x4 slice. The times are simulated.
32 devices in a mesh: ctx: 16 (over z, y, core), tp: 2 (over x).
Axes of the slice: x: 2, y: 2, z: 4, core: 2. Of those that a mesh axis runs over, the one named last changes fastest.
Arguments:
- tokens_clean: bfloat16 [2048, 4096], P(('ctx', 'tp')), may hold values from -6 to 6
- noise_mask: int32 [2048], P(('ctx', 'tp')), may hold values 0 or 1
- mask_embed: bfloat16 [4096], replicated, may hold values from -6 to 6
- norm_gain: bfloat16 [4096], replicated, may hold values from 0.099609375 to 1.8984375
- w_query: bfloat16 [4096, 2048], P(None, 'tp'), may hold values from -0.375 to 0.375
- w_key: bfloat16 [4096, 2048], P(None, 'tp'), may hold values from -0.375 to 0.375
- w_value: bfloat16 [4096, 2048], P(None, 'tp'), may hold values from -0.09375 to 0.09375
- w_out: bfloat16 [2048, 4096], P('tp'), may hold values from -0.5 to 0.5
- block_mask: int32 [64, 64], replicated, may hold values from 0 to 3, as said below
Outputs:
- clean_out: bfloat16 [2048, 4096], P(('ctx', 'tp'))
- noisy_out: bfloat16 [2048, 4096], P(('ctx', 'tp'))
Inputs may be any that keep to these rules, and one draw needn't show every extreme that they name: `block_mask`: entry (i, j) is a + 2 b: a = 1 where clean block i sees clean block j, b = 1 where noisy block i sees clean block j. For each i the j with a = 1 form one run ending at j = i, and those with b = 1 one run ending at j = i - 1, or none; entries with j > i are 0.
All inputs are finite; a program needn't handle non-finite values. No bound on the sum of `noise_mask` on one device may be relied on, other than what follows from the above.
Results may differ from a plain program's by a relative error of at most 0.014.
Values may be sent and summed in bfloat16 or wider, within the bound.
A program may use at most 128 MiB of HBM per device.

v0:
```python
import functools

import jax
import jax.numpy as jnp
import numpy as np
from jax import lax
from jax.experimental import pallas as pl
from jax.experimental.pallas import tpu as pltpu
from jax.sharding import PartitionSpec as P

HEAD_DIM = 128
BLOCK = 32


ROPE_BASE = 500000.0
EPSILON = 1e-05
NEG_FILL = -1e30


def rms_rows(values, gain):
    wide = values.astype(jnp.float32)
    factor = lax.rsqrt(jnp.mean(wide * wide, axis=-1, keepdims=True) + EPSILON)
    return (wide * factor * gain.astype(jnp.float32)).astype(jnp.bfloat16)


def rotate(values, positions):
    half_dim = values.shape[-1] // 2
    indices = jnp.arange(half_dim).astype(jnp.float32)
    freqs = ROPE_BASE ** (-2.0 * indices / values.shape[-1])
    angles = positions.astype(jnp.float32)[:, None] * freqs[None, :]
    cosine = jnp.cos(angles)[:, None, :]
    sine = jnp.sin(angles)[:, None, :]
    lower = values[..., :half_dim]
    upper = values[..., half_dim:]
    return jnp.concatenate([lower * cosine - upper * sine, upper * cosine + lower * sine], axis=-1)


def start_state(heads, length):
    return (
        jnp.full((heads, length), NEG_FILL, jnp.float32),
        jnp.zeros((heads, length), jnp.float32),
        jnp.zeros((heads, length, HEAD_DIM), jnp.float32),
    )


def attend(state, queries, keys, values, visible):
    peak_old, total_old, weighted_old = state
    scores = jnp.einsum(
        "qhd,khd->hqk", queries, keys, preferred_element_type=jnp.float32
    ) * HEAD_DIM ** (-0.5)
    scores = jnp.where(visible[None], scores, NEG_FILL)
    peak_new = jnp.maximum(peak_old, jnp.max(scores, axis=-1))
    weights = jnp.where(visible[None], jnp.exp(scores - peak_new[..., None]), 0.0)
    factor = jnp.exp(peak_old - peak_new)
    total_new = total_old * factor + jnp.sum(weights, axis=-1)
    weighted_new = weighted_old * factor[..., None] + jnp.einsum(
        "hqk,khd->hqd", weights.astype(jnp.bfloat16), values, preferred_element_type=jnp.float32
    )
    return (peak_new, total_new, weighted_new)


def local(
    tokens_clean, noise_mask, mask_embed, norm_gain, w_query, w_key, w_value, w_out, block_mask
):
    normed = rms_rows(tokens_clean, norm_gain)
    mask_row = rms_rows(mask_embed[None, :], norm_gain)
    gathered, noise_flags = (
        lax.all_gather(normed, "tp", axis=0, tiled=True),
        lax.all_gather(noise_mask, "tp", axis=0, tiled=True),
    )
    local_len = gathered.shape[0]
    width = w_query.shape[1]
    heads = width // HEAD_DIM
    first_row = lax.axis_index("ctx") * local_len
    positions = first_row + jnp.arange(local_len, dtype=jnp.int32)
    noisy_rows = (noise_flags == 1)[:, None]

    def project(weight, rotary):
        clean = jnp.dot(gathered, weight, preferred_element_type=jnp.float32)
        masked = jnp.dot(mask_row, weight, preferred_element_type=jnp.float32)
        noisy = jnp.where(noisy_rows, masked, clean)
        clean = clean.reshape(local_len, heads, HEAD_DIM)
        noisy = noisy.reshape(local_len, heads, HEAD_DIM)
        if rotary:
            clean = rotate(clean, positions)
            noisy = rotate(noisy, positions)
        return (clean.astype(jnp.bfloat16), noisy.astype(jnp.bfloat16))

    q_clean, q_noisy = project(w_query, True)
    k_clean, k_noisy = project(w_key, True)
    v_clean, v_noisy = project(w_value, False)
    key_values = jnp.stack([k_clean.reshape(local_len, width), v_clean.reshape(local_len, width)])

    def finish(state):
        weighted = state[2] / state[1][..., None]
        return jnp.transpose(weighted, (1, 0, 2)).reshape(local_len, width).astype(jnp.bfloat16)

    row_table = jnp.take(block_mask, positions // BLOCK, axis=0)
    own_block = (positions // BLOCK)[:, None] == (positions // BLOCK)[None, :]
    noisy_state = attend(start_state(heads, local_len), q_noisy, k_noisy, v_noisy, own_block)
    states = (start_state(heads, local_len), noisy_state)
    piece = lax.all_gather(key_values, "ctx", axis=1, tiled=True)
    count = piece.shape[1]
    visible = jnp.repeat(row_table, BLOCK, axis=1)
    keys = piece[0].reshape(count, heads, HEAD_DIM)
    values = piece[1].reshape(count, heads, HEAD_DIM)
    states = (
        attend(states[0], q_clean, keys, values, visible % 2 == 1),
        attend(states[1], q_noisy, keys, values, visible // 2 == 1),
    )
    attended = jnp.stack([finish(states[0]), finish(states[1])])
    model_width = w_out.shape[1]
    piece = attended
    summed = lax.psum_scatter(
        jnp.einsum("sqc,cd->qsd", piece, w_out, preferred_element_type=jnp.float32)
        .reshape(local_len // lax.axis_size("tp") * lax.axis_size("tp"), 2 * model_width)
        .astype(jnp.bfloat16),
        "tp",
        scatter_dimension=0,
        tiled=True,
    ).astype(jnp.float32)
    result = summed.reshape(summed.shape[0], 2, model_width)
    return (result[:, 0].astype(jnp.bfloat16), result[:, 1].astype(jnp.bfloat16))

LOG2E = 1.4426950408889634
MESH = pl.DeviceIdType.MESH


def layer_kernel(
    n_chips,
    x_ref, flag_ref, mask_ref, gain_ref, vis_ref, table_hbm, wq_hbm, wk_hbm, wv_hbm, wo_hbm,
    clean_ref, noisy_ref,
    w_s, wo_s, table, lhs0, lhs1, flag0, flag1, mproj, nb, sendq, sendkv, recvq, recvkv, kall, vall, bias,
    oown, lown, obuf, lbuf, oin, lin, att, psend, precv, pown,
    wsem, wosem, tsem, xs, xr, ss, sr, cs, cr, qs, qr, ls, lc, lq, fs, fr, os_, or_, es, er, ol, el, ps, pr,
):
    ctx = lax.axis_index("ctx")
    tp = lax.axis_index("tp")
    chip = ctx // 2
    core = ctx % 2
    rows = x_ref.shape[0]
    length = 2 * rows
    pairs = n_chips // 2
    hd = HEAD_DIM
    seq = 2 * n_chips * length
    per = length // BLOCK
    my_z = chip // 2
    w_hbm = (wq_hbm, wk_hbm, wv_hbm)
    twin = {"tp": 1 - tp}
    sibling = {"ctx": 2 * chip + 1 - core}

    def pair_at(i):
        return (my_z + 2 + i) % pairs

    def w_copy(kind, i):
        cols = pl.ds(pl.multiple_of(pair_at(i) * 2 * hd, 2 * hd), 2 * hd)
        return pltpu.make_async_copy(w_hbm[kind].at[:, cols], w_s.at[kind, :, cols], wsem.at[i, kind])

    def half_rows(half):
        which = tp if half == 0 else 1 - tp
        return pl.ds(pl.multiple_of(which * rows, rows), rows)

    table_copy = pltpu.make_async_copy(table_hbm.at[:, pl.ds(pl.multiple_of(ctx * length, length), length)], table, tsem)
    table_copy.start()
    for i in range(pairs):
        for kind in range(3):
            w_copy(kind, i).start()
    wo_copy = pltpu.make_async_copy(wo_hbm, wo_s, wosem)
    wo_copy.start()

    barrier = pltpu.get_barrier_semaphore()
    pl.semaphore_signal(barrier, inc=1, device_id=twin, device_id_type=MESH)
    pl.semaphore_signal(barrier, inc=1, device_id=sibling, device_id_type=MESH)
    for d in range(1, n_chips):
        peer = (chip + d) % n_chips
        pl.semaphore_signal(barrier, inc=1, device_id={"ctx": 2 * peer + core}, device_id_type=MESH)

    gain = gain_ref[...].reshape(1, x_ref.shape[1]).astype(jnp.float32)

    def norm(values):
        wide = values.astype(jnp.float32)
        factor = lax.rsqrt(jnp.mean(wide * wide, axis=-1, keepdims=True) + EPSILON)
        return (wide * factor * gain).astype(jnp.bfloat16)

    lhs0[0:rows, :] = norm(x_ref[...])
    lhs0[rows:rows + 16, :] = jnp.broadcast_to(norm(mask_ref[...].reshape(1, x_ref.shape[1])), (16, lhs0.shape[1]))
    flag0[...] = jnp.transpose(jnp.broadcast_to(flag_ref[...].astype(jnp.float32).reshape(1, rows), (hd, rows)))

    pl.semaphore_wait(barrier, n_chips + 1)

    def x_copy():
        return pltpu.make_async_remote_copy(
            src_ref=lhs0.at[pl.ds(0, rows)], dst_ref=lhs1, send_sem=xs.at[0], recv_sem=xr.at[0],
            device_id=twin, device_id_type=MESH)

    def flag_copy():
        return pltpu.make_async_remote_copy(
            src_ref=flag0, dst_ref=flag1, send_sem=xs.at[1], recv_sem=xr.at[1],
            device_id=twin, device_id_type=MESH)

    flag_copy().start()
    x_copy().start()

    def kv_copy(head, slot, half):
        where = half_rows(half)
        return pltpu.make_async_remote_copy(
            src_ref=sendkv.at[head, where], dst_ref=recvkv.at[slot, where],
            send_sem=ss.at[head, half], recv_sem=sr.at[slot, half],
            device_id={"ctx": 2 * head + core}, device_id_type=MESH)

    def clean_copy(head, slot, half):
        where = half_rows(half)
        return pltpu.make_async_remote_copy(
            src_ref=sendq.at[0, head, where], dst_ref=recvq.at[0, slot, where],
            send_sem=cs.at[head, half], recv_sem=cr.at[slot, half],
            device_id={"ctx": 2 * head + core}, device_id_type=MESH)

    def noisy_copy(head, slot):
        return pltpu.make_async_remote_copy(
            src_ref=sendq.at[1, head], dst_ref=recvq.at[1, slot], send_sem=qs.at[head], recv_sem=qr.at[slot],
            device_id={"ctx": 2 * head + core}, device_id_type=MESH)

    def kv_here(half):
        where = half_rows(half)
        return pltpu.make_async_copy(sendkv.at[chip, where], recvkv.at[chip, where], ls.at[half])

    def clean_here(half):
        where = half_rows(half)
        return pltpu.make_async_copy(sendq.at[0, chip, where], recvq.at[0, chip, where], lc.at[half])

    def noisy_here():
        return pltpu.make_async_copy(sendq.at[1, chip], recvq.at[1, chip], lq)

    key_at = lax.broadcasted_iota(jnp.int32, (vis_ref.shape[1], seq), 1)
    side = (key_at % (2 * length)) // length
    key_ctx = 2 * (key_at // (2 * length)) + jnp.where(side == 0, core, 1 - core)
    key_block = key_ctx * per + (key_at % length) // BLOCK
    spread = (lax.broadcasted_iota(jnp.int32, key_at.shape, 0) == key_block).astype(jnp.float32).astype(jnp.bfloat16)
    for copy in range(2):
        seen = ((vis_ref[...] >> copy) & 1).astype(jnp.float32).astype(jnp.bfloat16)
        shown = (jnp.dot(seen, spread, preferred_element_type=jnp.float32) - 1.0) * 1e30
        for c in range(2 * n_chips):
            bias[c, copy] = shown[c * per:(c + 1) * per]

    table_copy.wait()
    for half in range(2):
        if half == 1:
            flag_copy().wait_recv()
            x_copy().wait_recv()
        where = half_rows(half)

        def project(i, carry):
            pair = pair_at(i)
            cols = pl.ds(pl.multiple_of(pair * 2 * hd, 2 * hd), 2 * hd)
            if half == 0:
                for kind in range(3):
                    w_copy(kind, i).wait()
            flags = (flag0 if half == 0 else flag1)[...]
            cosine = table[0, where]
            sine = table[1, where]
            for kind in (1, 2, 0):
                left = (lhs0 if half == 0 else lhs1)[...]
                result = jnp.dot(left, w_s[kind, :, cols], preferred_element_type=jnp.float32)
                if half == 0:
                    mproj[kind, :, cols] = result[rows:rows + 8]
                    masked = result[rows:rows + 1]
                else:
                    masked = mproj[kind, :, cols][0:1]
                clean2 = result[0:rows]
                for k in range(2):
                    head = 2 * pair + k
                    clean = clean2[:, k * hd:(k + 1) * hd]
                    noisy = jnp.where(flags == 1.0, masked[:, k * hd:(k + 1) * hd], clean)
                    if kind < 2:
                        clean = clean * cosine + pltpu.roll(clean, hd // 2, 1) * sine
                        noisy = noisy * cosine + pltpu.roll(noisy, hd // 2, 1) * sine
                    clean = clean.astype(jnp.bfloat16)
                    noisy = noisy.astype(jnp.bfloat16)
                    if kind == 0:
                        sendq[0, head, where, :] = clean
                        sendq[1, head, where, :] = noisy
                    else:
                        nb[kind - 1, head, where, :] = noisy
                        sendkv[head, where, (kind - 1) * hd:kind * hd] = clean
                if kind != 1:
                    for k in range(2):
                        head = 2 * pair + k

                        @pl.when(head != chip)
                        def _():
                            (clean_copy if kind == 0 else kv_copy)(head, chip, half).start()

                        @pl.when(head == chip)
                        def _():
                            (clean_here if kind == 0 else kv_here)(half).start()
            return carry

        lax.fori_loop(0, pairs, project, 0)

    for d in range(1, n_chips):
        noisy_copy((chip + d) % n_chips, chip).start()
    noisy_here().start()

    scale = LOG2E * hd ** -0.5
    own = (lax.broadcasted_iota(jnp.int32, (length, length), 0) // BLOCK
           == lax.broadcasted_iota(jnp.int32, (length, length), 1) // BLOCK)

    def dot_t(a, b):
        return lax.dot_general(a, b, (((1,), (1,)), ((), ())), preferred_element_type=jnp.float32)

    for head in range(n_chips):
        scores = jnp.where(own, dot_t(sendq[1, head], nb[0, head]) * scale, NEG_FILL)
        peak = jnp.max(scores, axis=-1, keepdims=True)
        weights = jnp.exp2(scores - peak)
        total = jnp.sum(weights, axis=-1, keepdims=True)
        oown[head] = jnp.dot(weights.astype(jnp.bfloat16), nb[1, head], preferred_element_type=jnp.float32) / total
        lown[head] = jnp.broadcast_to(peak + jnp.log(total) * LOG2E, (length, hd))

    def share(p, kind):
        return pltpu.make_async_remote_copy(
            src_ref=recvkv.at[p, :, pl.ds(kind * hd, hd)],
            dst_ref=(kall, vall)[kind].at[p, pl.ds(length, length)],
            send_sem=fs.at[p, kind], recv_sem=fr.at[p, kind],
            device_id=sibling, device_id_type=MESH)

    def back(p, copy, slot):
        return pltpu.make_async_remote_copy(
            src_ref=obuf.at[copy, p], dst_ref=oin.at[copy, slot], send_sem=os_.at[copy, p], recv_sem=or_.at[copy, slot],
            device_id={"ctx": 2 * p + core}, device_id_type=MESH)

    def level_back(p, slot):
        return pltpu.make_async_remote_copy(
            src_ref=lbuf.at[p], dst_ref=lin.at[slot], send_sem=es.at[p], recv_sem=er.at[slot],
            device_id={"ctx": 2 * p + core}, device_id_type=MESH)

    def back_here(copy):
        return pltpu.make_async_copy(obuf.at[copy, chip], oin.at[copy, chip], ol.at[copy])

    def level_here():
        return pltpu.make_async_copy(lbuf.at[chip], lin.at[chip], el)

    for p in range(n_chips):
        for half in range(2):
            @pl.when(chip != p)
            def _():
                kv_copy(p, p, half).wait_recv()

            @pl.when(chip == p)
            def _():
                kv_here(half).wait()
        for kind in range(2):
            share(p, kind).start()
        kall[p, 0:length, :] = recvkv[p, :, 0:hd]
        vall[p, 0:length, :] = recvkv[p, :, hd:2 * hd]
    for p in range(n_chips):
        for kind in range(2):
            share(p, kind).wait_recv()

    chunks = psend.shape[1]
    width = psend.shape[3]

    def term_copy(copy, j):
        return pltpu.make_async_remote_copy(
            src_ref=psend.at[copy, j], dst_ref=precv.at[copy, j], send_sem=ps.at[copy, j], recv_sem=pr.at[copy, j],
            device_id=twin, device_id_type=MESH)

    def out_cols(j):
        return pl.ds(pl.multiple_of(j * width, width), width)

    def project_out(copy):
        mine = half_rows(0)
        theirs = half_rows(1)
        for head in range(n_chips):
            @pl.when(chip != head)
            def _():
                back(head, copy, head).wait_recv()

            @pl.when(chip == head)
            def _():
                back_here(copy).wait()
            if copy == 1:
                @pl.when(chip != head)
                def _():
                    level_back(head, head).wait_recv()

                @pl.when(chip == head)
                def _():
                    level_here().wait()
                away = jnp.transpose(jnp.broadcast_to(lin[head][0:1], (length, hd)))
                home = lown[head]
                top = jnp.maximum(away, home)
                w_away = jnp.exp2(away - top)
                w_home = jnp.exp2(home - top)
                noisy = oin[1, head].astype(jnp.float32)
                noisy = (noisy * w_away + oown[head] * w_home) / (w_away + w_home)
                oin[1, head] = noisy.astype(jnp.bfloat16)
            cols = slice(head * hd, (head + 1) * hd)
            att[copy, 0:rows, cols] = oin[copy, head, theirs, :]
            att[copy, rows:length, cols] = oin[copy, head, mine, :]

        def term(j, carry):
            both = jnp.dot(att[copy], wo_s[:, out_cols(j)], preferred_element_type=jnp.float32).astype(jnp.bfloat16)
            psend[copy, j] = both[0:rows]
            pown[copy, j] = both[rows:length]
            term_copy(copy, j).start()
            return carry

        lax.fori_loop(0, chunks, term, 0)

    def attend_step(step, carry):
        copy = step // n_chips
        p = (chip + step) % n_chips

        @pl.when((copy == 0) & (chip != p))
        def _():
            for half in range(2):
                clean_copy(p, p, half).wait_recv()

        @pl.when((copy == 0) & (chip == p))
        def _():
            for half in range(2):
                clean_here(half).wait()

        @pl.when((copy == 1) & (chip != p))
        def _():
            noisy_copy(p, p).wait_recv()

        @pl.when((copy == 1) & (chip == p))
        def _():
            noisy_here().wait()

        for k in range(n_chips):
            @pl.when(p == k)
            def _():
                count = (k + 1) * 2 * length
                keys = kall[0:k + 1].reshape(count, hd)
                values = vall[0:k + 1].reshape(count, hd)
                shown = bias[2 * k + core, copy][:, 0:count]
                queries = recvq[copy, k]
                extra = jnp.concatenate(
                    [jnp.broadcast_to(shown[b:b + 1], (BLOCK, count)) for b in range(per)], axis=0)
                scores = dot_t(queries, keys) * scale + extra
                peak = jnp.max(scores, axis=-1, keepdims=True)
                weights = jnp.exp2(scores - peak)
                total = jnp.sum(weights, axis=-1, keepdims=True)
                result = jnp.dot(weights.astype(jnp.bfloat16), values, preferred_element_type=jnp.float32) / total
                obuf[copy, k] = result.astype(jnp.bfloat16)

                @pl.when(copy == 1)
                def _():
                    level = jnp.broadcast_to(peak + jnp.log(total) * LOG2E, (length, hd))
                    lbuf[k] = jnp.transpose(level)[0:8]

        @pl.when(chip != p)
        def _():
            back(p, copy, chip).start()

        @pl.when(chip == p)
        def _():
            back_here(copy).start()

        @pl.when((copy == 1) & (chip != p))
        def _():
            level_back(p, chip).start()

        @pl.when((copy == 1) & (chip == p))
        def _():
            level_here().start()

        @pl.when(step == n_chips + n_chips // 2 - 1)
        def _():
            wo_copy.wait()
            project_out(0)
        return carry

    lax.fori_loop(0, 2 * n_chips, attend_step, 0)
    project_out(1)

    for copy, out_ref in ((0, clean_ref), (1, noisy_ref)):
        def total_of(j, carry):
            term_copy(copy, j).wait_recv()
            out_ref[:, out_cols(j)] = pown[copy, j].astype(jnp.float32) + precv[copy, j].astype(jnp.float32)
            return carry

        lax.fori_loop(0, chunks, total_of, 0)

    flag_copy().wait_send()
    x_copy().wait_send()
    for p in range(n_chips):
        for kind in range(2):
            share(p, kind).wait_send()

        @pl.when(chip != p)
        def _():
            for half in range(2):
                kv_copy(p, chip, half).wait_send()
                clean_copy(p, chip, half).wait_send()
            noisy_copy(p, chip).wait_send()
            for copy in range(2):
                back(p, copy, chip).wait_send()
            level_back(p, chip).wait_send()
    for copy in range(2):
        for j in range(chunks):
            term_copy(copy, j).wait_send()


def rotary_table(length):
    indices = np.arange(HEAD_DIM // 2).astype(np.float32)
    freqs = (ROPE_BASE ** (-2.0 * indices.astype(np.float64) / HEAD_DIM)).astype(np.float32)
    angles = (np.arange(length, dtype=np.float32)[:, None] * freqs[None, :]).astype(np.float64)
    cosine = np.cos(angles).astype(np.float32)
    sine = np.sin(angles).astype(np.float32)
    return np.stack([np.concatenate([cosine, cosine], axis=1), np.concatenate([-sine, sine], axis=1)])


def local_kernel(
    tokens_clean, noise_mask, mask_embed, norm_gain, w_query, w_key, w_value, w_out, block_mask
):
    rows, model = tokens_clean.shape
    length = 2 * rows
    width = w_query.shape[1]
    n_chips = width // HEAD_DIM
    hd = HEAD_DIM
    seq = 2 * n_chips * length
    per = length // BLOCK
    bf, f32 = jnp.bfloat16, jnp.float32
    chunks = 8
    part = model // chunks
    dma = pltpu.SemaphoreType.DMA
    vmem = pl.BlockSpec(memory_space=pltpu.VMEM)
    hbm = pl.BlockSpec(memory_space=pl.ANY)
    clean, noisy = pl.pallas_call(
        functools.partial(layer_kernel, n_chips),
        out_shape=(jax.ShapeDtypeStruct((rows, model), f32), jax.ShapeDtypeStruct((rows, model), f32)),
        in_specs=[vmem] * 5 + [hbm] * 5,
        out_specs=(vmem, vmem),
        scratch_shapes=[
            pltpu.VMEM((3, model, width), bf),
            pltpu.VMEM((width, model), bf),
            pltpu.VMEM((2, length, hd), f32),
            pltpu.VMEM((rows + 16, model), bf),
            pltpu.VMEM((rows, model), bf),
            pltpu.VMEM((rows, hd), f32),
            pltpu.VMEM((rows, hd), f32),
            pltpu.VMEM((3, 8, width), f32),
            pltpu.VMEM((2, n_chips, length, hd), bf),
            pltpu.VMEM((2, n_chips, length, hd), bf),
            pltpu.VMEM((n_chips, length, 2 * hd), bf),
            pltpu.VMEM((2, n_chips, length, hd), bf),
            pltpu.VMEM((n_chips, length, 2 * hd), bf),
            pltpu.VMEM((n_chips, 2 * length, hd), bf),
            pltpu.VMEM((n_chips, 2 * length, hd), bf),
            pltpu.VMEM((2 * n_chips, 2, per, seq), f32),
            pltpu.VMEM((n_chips, length, hd), f32),
            pltpu.VMEM((n_chips, length, hd), f32),
            pltpu.VMEM((2, n_chips, length, hd), bf),
            pltpu.VMEM((n_chips, 8, hd), f32),
            pltpu.VMEM((2, n_chips, length, hd), bf),
            pltpu.VMEM((n_chips, 8, hd), f32),
            pltpu.VMEM((2, length, width), bf),
            pltpu.VMEM((2, chunks, rows, part), bf),
            pltpu.VMEM((2, chunks, rows, part), bf),
            pltpu.VMEM((2, chunks, rows, part), bf),
            dma((n_chips // 2, 3)),
            dma,
            dma,
            dma((2,)),
            dma((2,)),
            dma((n_chips, 2)),
            dma((n_chips, 2)),
            dma((n_chips, 2)),
            dma((n_chips, 2)),
            dma((n_chips,)),
            dma((n_chips,)),
            dma((2,)),
            dma((2,)),
            dma,
            dma((n_chips, 2)),
            dma((n_chips, 2)),
            dma((2, n_chips)),
            dma((2, n_chips)),
            dma((n_chips,)),
            dma((n_chips,)),
            dma((2,)),
            dma,
            dma((2, chunks)),
            dma((2, chunks)),
        ],
        compiler_params=pltpu.CompilerParams(
            collective_id=0, has_side_effects=True, vmem_limit_bytes=60 * 1024 * 1024),
        cost_estimate=pl.CostEstimate(flops=6 * 10**9, bytes_accessed=34 * 2**20, transcendentals=3 * 10**6),
    )(tokens_clean, noise_mask, mask_embed, norm_gain, block_mask, jnp.asarray(rotary_table(seq)),
      w_query, w_key, w_value, w_out)
    return (clean.astype(bf), noisy.astype(bf))


def fits(mesh, tokens_clean, w_query):
    n_ctx, n_tp = mesh.shape["ctx"], mesh.shape["tp"]
    heads = w_query.shape[1] // n_tp // HEAD_DIM
    tokens = tokens_clean.shape[0] // n_ctx
    return n_tp == 2 and n_ctx == 2 * heads and heads % 4 == 0 and tokens == HEAD_DIM


def solution(mesh):
    specs = dict(
        mesh=mesh,
        in_specs=(
            P(("ctx", "tp"), None),
            P(("ctx", "tp")),
            P(),
            P(),
            P(None, "tp"),
            P(None, "tp"),
            P(None, "tp"),
            P("tp", None),
            P(),
        ),
        out_specs=(P(("ctx", "tp"), None), P(("ctx", "tp"), None)),
        check_vma=False,
    )

    def layer(tokens_clean, noise_mask, mask_embed, norm_gain, w_query, w_key, w_value, w_out, block_mask):
        body = local_kernel if fits(mesh, tokens_clean, w_query) else local
        return jax.shard_map(body, **specs)(
            tokens_clean, noise_mask, mask_embed, norm_gain, w_query, w_key, w_value, w_out, block_mask)

    return layer
```

profile of v0, /device:TPU:0, one launch (start us, length us, event | category | flops | bytes accessed | tf_op | source)
XLA Modules:
  0.0 74.3 jit_solution(11631244910302096604)
XLA Ops:
  0.6 69.5 %shard_map.113 = (f32[64,4096]{1,0:T(8,128)}, f32[64,4096]{1,0:T(8,128)}) custom-call(bf16[64,4096]{1,0:T(8,128)(2,1)} %x_ref.1, s32[64]{0:T(128)} %flag_ref.1, bf16[4096]{0:T(1024)(128)(2,1)} %mask_ref.1, bf16[4096]{0:T(1024)(128)(2,1)} %gain_ref.1, s32[64,64]{1,0:T(8,128)} %vis_ref.1, f32[2,2048,128]{2,1,0:T(8,128)} %constant.2.clone.table_hbm, ...), custom_call_target="tpu_custom_call" | custom-call | flops 6000000000 | bytes 35651584 | tf_op jit(solution)/shard_map/pallas_call | solution.py:532
  70.2 2.1 %convert_element_type.6 = bf16[64,4096]{1,0:T(8,128)(2,1)} convert(f32[64,4096]{1,0:T(8,128)} %get-tuple-element.4) | non-fusion elementwise | flops 262144 | bytes 1572864 | tf_op jit(solution)/shard_map/convert_element_type | solution.py:594
  72.3 2.1 %convert_element_type.7 = bf16[64,4096]{1,0:T(8,128)(2,1)} convert(f32[64,4096]{1,0:T(8,128)} %get-tuple-element.5) | non-fusion elementwise | flops 262144 | bytes 1572864 | tf_op jit(solution)/shard_map/convert_element_type | solution.py:594
where the time goes:
time: 74.5 us; the launch traced here: 74.3 us
  Pallas kernels  69.5 us (93%)
  other arithmetic  4.14 us (6%)
    pallas_call x1, Pallas kernels, local_kernel(): pl.pallas_call(functools.partial(layer_kernel, n_chips), out_shape=(jax.S...  69.5 us
    convert_element_type x2, other arithmetic, local_kernel(): return (clean.astype(bf), noisy.astype(bf))  4.14 us

commit v1 on v0

--- a/solution.py
+++ b/solution.py
@@ -129,10 +129,10 @@
 def layer_kernel(
     n_chips,
     x_ref, flag_ref, mask_ref, gain_ref, vis_ref, table_hbm, wq_hbm, wk_hbm, wv_hbm, wo_hbm,
-    clean_ref, noisy_ref,
-    w_s, wo_s, table, lhs0, lhs1, flag0, flag1, mproj, nb, sendq, sendkv, recvq, recvkv, kall, vall, bias,
+    out_ref,
+    w_s, wo_s, table, lhs0, lhs1, row0, row1, flags, rowall, rowin, mproj, nb, sendq, sendkv, recvq, recvkv, kall, vall, bias,
     oown, lown, obuf, lbuf, oin, lin, att, psend, precv, pown,
-    wsem, wosem, tsem, xs, xr, ss, sr, cs, cr, qs, qr, ls, lc, lq, fs, fr, os_, or_, es, er, ol, el, ps, pr,
+    wsem, wosem, tsem, xs, xr, ss, sr, cs, cr, gs, gr, ls, lc, lg, fs, fr, os_, or_, es, er, ol, el, ps, pr,
 ):
     ctx = lax.axis_index("ctx")
     tp = lax.axis_index("tp")
@@ -160,11 +160,12 @@
         which = tp if half == 0 else 1 - tp
         return pl.ds(pl.multiple_of(which * rows, rows), rows)
 
-    table_copy = pltpu.make_async_copy(table_hbm.at[:, pl.ds(pl.multiple_of(ctx * length, length), length)], table, tsem)
-    table_copy.start()
+    table_copy = pltpu.make_async_copy(table_hbm, table, tsem)
     for i in range(pairs):
-        for kind in range(3):
+        for kind in (1, 2, 0):
             w_copy(kind, i).start()
+        if i == 0:
+            table_copy.start()
     wo_copy = pltpu.make_async_copy(wo_hbm, wo_s, wosem)
     wo_copy.start()
 
@@ -184,7 +185,8 @@
 
     lhs0[0:rows, :] = norm(x_ref[...])
     lhs0[rows:rows + 16, :] = jnp.broadcast_to(norm(mask_ref[...].reshape(1, x_ref.shape[1])), (16, lhs0.shape[1]))
-    flag0[...] = jnp.transpose(jnp.broadcast_to(flag_ref[...].astype(jnp.float32).reshape(1, rows), (hd, rows)))
+    flag_row = flag_ref[...].astype(jnp.float32).reshape(1, rows)
+    row0[...] = jnp.broadcast_to(jnp.concatenate([flag_row, flag_row], axis=1), row0.shape)
 
     pl.semaphore_wait(barrier, n_chips + 1)
 
@@ -195,7 +197,7 @@
 
     def flag_copy():
         return pltpu.make_async_remote_copy(
-            src_ref=flag0, dst_ref=flag1, send_sem=xs.at[1], recv_sem=xr.at[1],
+            src_ref=row0, dst_ref=row1, send_sem=xs.at[1], recv_sem=xr.at[1],
             device_id=twin, device_id_type=MESH)
 
     flag_copy().start()
@@ -215,9 +217,9 @@
             send_sem=cs.at[head, half], recv_sem=cr.at[slot, half],
             device_id={"ctx": 2 * head + core}, device_id_type=MESH)
 
-    def noisy_copy(head, slot):
-        return pltpu.make_async_remote_copy(
-            src_ref=sendq.at[1, head], dst_ref=recvq.at[1, slot], send_sem=qs.at[head], recv_sem=qr.at[slot],
+    def row_copy(head, slot):
+        return pltpu.make_async_remote_copy(
+            src_ref=rowall, dst_ref=rowin.at[slot], send_sem=gs.at[head], recv_sem=gr.at[slot],
             device_id={"ctx": 2 * head + core}, device_id_type=MESH)
 
     def kv_here(half):
@@ -228,24 +230,23 @@
         where = half_rows(half)
         return pltpu.make_async_copy(sendq.at[0, chip, where], recvq.at[0, chip, where], lc.at[half])
 
-    def noisy_here():
-        return pltpu.make_async_copy(sendq.at[1, chip], recvq.at[1, chip], lq)
-
-    key_at = lax.broadcasted_iota(jnp.int32, (vis_ref.shape[1], seq), 1)
-    side = (key_at % (2 * length)) // length
-    key_ctx = 2 * (key_at // (2 * length)) + jnp.where(side == 0, core, 1 - core)
-    key_block = key_ctx * per + (key_at % length) // BLOCK
-    spread = (lax.broadcasted_iota(jnp.int32, key_at.shape, 0) == key_block).astype(jnp.float32).astype(jnp.bfloat16)
-    for copy in range(2):
-        seen = ((vis_ref[...] >> copy) & 1).astype(jnp.float32).astype(jnp.bfloat16)
-        shown = (jnp.dot(seen, spread, preferred_element_type=jnp.float32) - 1.0) * 1e30
-        for c in range(2 * n_chips):
-            bias[c, copy] = shown[c * per:(c + 1) * per]
+    def row_here():
+        return pltpu.make_async_copy(rowall, rowin.at[chip], lg)
+
+    def column(row):
+        return jnp.transpose(jnp.broadcast_to(row, (length, length)))
+
+    flag_copy().wait_recv()
+    lane = lax.broadcasted_iota(jnp.int32, row0.shape, 1)
+    rowall[...] = jnp.where(lane // rows == tp, row0[...], row1[...])
+    for d in range(1, n_chips):
+        row_copy((chip + d) % n_chips, chip).start()
+    row_here().start()
+    flags[...] = column(rowall[0:1])
 
     table_copy.wait()
     for half in range(2):
         if half == 1:
-            flag_copy().wait_recv()
             x_copy().wait_recv()
         where = half_rows(half)
 
@@ -255,9 +256,10 @@
             if half == 0:
                 for kind in range(3):
                     w_copy(kind, i).wait()
-            flags = (flag0 if half == 0 else flag1)[...]
-            cosine = table[0, where]
-            sine = table[1, where]
+            flag = flags[where]
+            token_rows = pl.ds(pl.multiple_of(ctx * length + (tp if half == 0 else 1 - tp) * rows, rows), rows)
+            cosine = table[0, token_rows]
+            sine = table[1, token_rows]
             for kind in (1, 2, 0):
                 left = (lhs0 if half == 0 else lhs1)[...]
                 result = jnp.dot(left, w_s[kind, :, cols], preferred_element_type=jnp.float32)
@@ -270,7 +272,7 @@
                 for k in range(2):
                     head = 2 * pair + k
                     clean = clean2[:, k * hd:(k + 1) * hd]
-                    noisy = jnp.where(flags == 1.0, masked[:, k * hd:(k + 1) * hd], clean)
+                    noisy = jnp.where(flag == 1.0, masked[:, k * hd:(k + 1) * hd], clean)
                     if kind < 2:
                         clean = clean * cosine + pltpu.roll(clean, hd // 2, 1) * sine
                         noisy = noisy * cosine + pltpu.roll(noisy, hd // 2, 1) * sine
@@ -297,9 +299,16 @@
 
         lax.fori_loop(0, pairs, project, 0)
 
-    for d in range(1, n_chips):
-        noisy_copy((chip + d) % n_chips, chip).start()
-    noisy_here().start()
+    key_at = lax.broadcasted_iota(jnp.int32, (vis_ref.shape[1], seq), 1)
+    side = (key_at % (2 * length)) // length
+    key_ctx = 2 * (key_at // (2 * length)) + jnp.where(side == 0, core, 1 - core)
+    key_block = key_ctx * per + (key_at % length) // BLOCK
+    spread = (lax.broadcasted_iota(jnp.int32, key_at.shape, 0) == key_block).astype(jnp.float32).astype(jnp.bfloat16)
+    for copy in range(2):
+        seen = ((vis_ref[...] >> copy) & 1).astype(jnp.float32).astype(jnp.bfloat16)
+        shown = (jnp.dot(seen, spread, preferred_element_type=jnp.float32) - 1.0) * 1e30
+        for c in range(2 * n_chips):
+            bias[c, copy] = shown[c * per:(c + 1) * per]
 
     scale = LOG2E * hd ** -0.5
     own = (lax.broadcasted_iota(jnp.int32, (length, length), 0) // BLOCK
@@ -330,14 +339,14 @@
 
     def level_back(p, slot):
         return pltpu.make_async_remote_copy(
-            src_ref=lbuf.at[p], dst_ref=lin.at[slot], send_sem=es.at[p], recv_sem=er.at[slot],
+            src_ref=lbuf.at[1, p], dst_ref=lin.at[slot], send_sem=es.at[p], recv_sem=er.at[slot],
             device_id={"ctx": 2 * p + core}, device_id_type=MESH)
 
     def back_here(copy):
         return pltpu.make_async_copy(obuf.at[copy, chip], oin.at[copy, chip], ol.at[copy])
 
     def level_here():
-        return pltpu.make_async_copy(lbuf.at[chip], lin.at[chip], el)
+        return pltpu.make_async_copy(lbuf.at[1, chip], lin.at[chip], el)
 
     for p in range(n_chips):
         for half in range(2):
@@ -408,78 +417,80 @@
         lax.fori_loop(0, chunks, term, 0)
 
     def attend_step(step, carry):
-        copy = step // n_chips
-        p = (chip + step) % n_chips
-
-        @pl.when((copy == 0) & (chip != p))
-        def _():
-            for half in range(2):
-                clean_copy(p, p, half).wait_recv()
-
-        @pl.when((copy == 0) & (chip == p))
-        def _():
-            for half in range(2):
-                clean_here(half).wait()
-
-        @pl.when((copy == 1) & (chip != p))
-        def _():
-            noisy_copy(p, p).wait_recv()
-
-        @pl.when((copy == 1) & (chip == p))
-        def _():
-            noisy_here().wait()
-
-        for k in range(n_chips):
-            @pl.when(p == k)
-            def _():
-                count = (k + 1) * 2 * length
-                keys = kall[0:k + 1].reshape(count, hd)
-                values = vall[0:k + 1].reshape(count, hd)
-                shown = bias[2 * k + core, copy][:, 0:count]
-                queries = recvq[copy, k]
-                extra = jnp.concatenate(
-                    [jnp.broadcast_to(shown[b:b + 1], (BLOCK, count)) for b in range(per)], axis=0)
-                scores = dot_t(queries, keys) * scale + extra
-                peak = jnp.max(scores, axis=-1, keepdims=True)
-                weights = jnp.exp2(scores - peak)
-                total = jnp.sum(weights, axis=-1, keepdims=True)
-                result = jnp.dot(weights.astype(jnp.bfloat16), values, preferred_element_type=jnp.float32) / total
-                obuf[copy, k] = result.astype(jnp.bfloat16)
-
-                @pl.when(copy == 1)
-                def _():
+        copy = step // pairs
+        low = (my_z + step) % pairs
+        chosen = (low, n_chips - 1 - low)
+        for p in chosen:
+            @pl.when((copy == 0) & (chip != p))
+            def _():
+                for half in range(2):
+                    clean_copy(p, p, half).wait_recv()
+                row_copy(p, p).wait_recv()
+
+            @pl.when((copy == 0) & (chip == p))
+            def _():
+                for half in range(2):
+                    clean_here(half).wait()
+                row_here().wait()
+
+            @pl.when(copy == 1)
+            def _():
+                token_rows = pl.ds(pl.multiple_of((2 * p + core) * length, length), length)
+                masked = jnp.broadcast_to(mproj[0, :, pl.ds(pl.multiple_of(chip * hd, hd), hd)][0:1], (length, hd))
+                masked = masked * table[0, token_rows] + pltpu.roll(masked, hd // 2, 1) * table[1, token_rows]
+                clean = recvq[0, p].astype(jnp.float32)
+                recvq[1, p] = jnp.where(column(rowin[p][0:1]) == 1.0, masked, clean).astype(jnp.bfloat16)
+
+        for k in range(pairs):
+            @pl.when(low == k)
+            def _():
+                for q in (k, n_chips - 1 - k):
+                    count = (q + 1) * 2 * length
+                    keys = kall[0:q + 1].reshape(count, hd)
+                    values = vall[0:q + 1].reshape(count, hd)
+                    shown = bias[2 * q + core, copy][:, 0:count]
+                    extra = jnp.concatenate(
+                        [jnp.broadcast_to(shown[b:b + 1], (BLOCK, count)) for b in range(per)], axis=0)
+                    scores = dot_t(recvq[copy, q], keys) * scale + extra
+                    peak = jnp.max(scores, axis=-1, keepdims=True)
+                    weights = jnp.exp2(scores - peak)
+                    total = jnp.sum(weights, axis=-1, keepdims=True)
+                    result = jnp.dot(weights.astype(jnp.bfloat16), values, preferred_element_type=jnp.float32) / total
+                    obuf[copy, q] = result.astype(jnp.bfloat16)
                     level = jnp.broadcast_to(peak + jnp.log(total) * LOG2E, (length, hd))
-                    lbuf[k] = jnp.transpose(level)[0:8]
-
-        @pl.when(chip != p)
-        def _():
-            back(p, copy, chip).start()
-
-        @pl.when(chip == p)
-        def _():
-            back_here(copy).start()
-
-        @pl.when((copy == 1) & (chip != p))
-        def _():
-            level_back(p, chip).start()
-
-        @pl.when((copy == 1) & (chip == p))
-        def _():
-            level_here().start()
-
-        @pl.when(step == n_chips + n_chips // 2 - 1)
+                    lbuf[copy, q] = jnp.transpose(level)[0:8]
+
+        for p in chosen:
+            @pl.when(chip != p)
+            def _():
+                back(p, copy, chip).start()
+
+            @pl.when(chip == p)
+            def _():
+                back_here(copy).start()
+
+            @pl.when((copy == 1) & (chip != p))
+            def _():
+                level_back(p, chip).start()
+
+            @pl.when((copy == 1) & (chip == p))
+            def _():
+                level_here().start()
+
+        @pl.when(step == pairs + pairs // 2 - 1)
         def _():
             wo_copy.wait()
             project_out(0)
         return carry
 
-    lax.fori_loop(0, 2 * n_chips, attend_step, 0)
+    lax.fori_loop(0, 2 * pairs, attend_step, 0)
     project_out(1)
 
-    for copy, out_ref in ((0, clean_ref), (1, noisy_ref)):
+    for copy in range(2):
         def total_of(j, carry):
             term_copy(copy, j).wait_recv()
-            out_ref[:, out_cols(j)] = pown[copy, j].astype(jnp.float32) + precv[copy, j].astype(jnp.float32)
+            summed = pown[copy, j].astype(jnp.float32) + precv[copy, j].astype(jnp.float32)
+            out_ref[copy, :, out_cols(j)] = summed.astype(jnp.bfloat16)
             return carry
 
         lax.fori_loop(0, chunks, total_of, 0)
@@ -495,13 +506,25 @@
             for half in range(2):
                 kv_copy(p, chip, half).wait_send()
                 clean_copy(p, chip, half).wait_send()
-            noisy_copy(p, chip).wait_send()
+            row_copy(p, chip).wait_send()
             for copy in range(2):
                 back(p, copy, chip).wait_send()
             level_back(p, chip).wait_send()
     for copy in range(2):
         for j in range(chunks):
             term_copy(copy, j).wait_send()
+
+
+def place_kernel(both, clean, noisy, sems):
+    half = clean.shape[0] // 2
+    copies = [
+        pltpu.make_async_copy(both.at[c, pl.ds(h * half, half)], out.at[pl.ds(h * half, half)], sems.at[c, h])
+        for c, out in enumerate((clean, noisy)) for h in range(2)
+    ]
+    for copy in copies:
+        copy.start()
+    for copy in copies:
+        copy.wait()
 
 
 def rotary_table(length):
@@ -529,19 +552,22 @@
     dma = pltpu.SemaphoreType.DMA
     vmem = pl.BlockSpec(memory_space=pltpu.VMEM)
     hbm = pl.BlockSpec(memory_space=pl.ANY)
-    clean, noisy = pl.pallas_call(
+    both = pl.pallas_call(
         functools.partial(layer_kernel, n_chips),
-        out_shape=(jax.ShapeDtypeStruct((rows, model), f32), jax.ShapeDtypeStruct((rows, model), f32)),
+        out_shape=jax.ShapeDtypeStruct((2, rows, model), bf),
         in_specs=[vmem] * 5 + [hbm] * 5,
-        out_specs=(vmem, vmem),
+        out_specs=vmem,
         scratch_shapes=[
             pltpu.VMEM((3, model, width), bf),
             pltpu.VMEM((width, model), bf),
-            pltpu.VMEM((2, length, hd), f32),
+            pltpu.VMEM((2, seq, hd), f32),
             pltpu.VMEM((rows + 16, model), bf),
             pltpu.VMEM((rows, model), bf),
-            pltpu.VMEM((rows, hd), f32),
-            pltpu.VMEM((rows, hd), f32),
+            pltpu.VMEM((8, length), f32),
+            pltpu.VMEM((8, length), f32),
+            pltpu.VMEM((length, hd), f32),
+            pltpu.VMEM((8, length), f32),
+            pltpu.VMEM((n_chips, 8, length), f32),
             pltpu.VMEM((3, 8, width), f32),
             pltpu.VMEM((2, n_chips, length, hd), bf),
             pltpu.VMEM((2, n_chips, length, hd), bf),
@@ -554,7 +580,7 @@
             pltpu.VMEM((n_chips, length, hd), f32),
             pltpu.VMEM((n_chips, length, hd), f32),
             pltpu.VMEM((2, n_chips, length, hd), bf),
-            pltpu.VMEM((n_chips, 8, hd), f32),
+            pltpu.VMEM((2, n_chips, 8, hd), f32),
             pltpu.VMEM((2, n_chips, length, hd), bf),
             pltpu.VMEM((n_chips, 8, hd), f32),
             pltpu.VMEM((2, length, width), bf),
@@ -591,7 +617,13 @@
         cost_estimate=pl.CostEstimate(flops=6 * 10**9, bytes_accessed=34 * 2**20, transcendentals=3 * 10**6),
     )(tokens_clean, noise_mask, mask_embed, norm_gain, block_mask, jnp.asarray(rotary_table(seq)),
       w_query, w_key, w_value, w_out)
-    return (clean.astype(bf), noisy.astype(bf))
+    return pl.pallas_call(
+        place_kernel,
+        out_shape=(jax.ShapeDtypeStruct((rows, model), bf), jax.ShapeDtypeStruct((rows, model), bf)),
+        in_specs=[hbm],
+        out_specs=(hbm, hbm),
+        scratch_shapes=[dma((2, 2))],
+    )(both)
 
 
 def fits(mesh, tokens_clean, w_query):

time: 74.5 us -> 102 us (1.37)
  Pallas kernels: 69.5 us -> 101 us
  other arithmetic: 4.14 us -> 0 us
    pallas_call x1 -> x2, Pallas kernels: 69.5 us -> 101 us  [the longest x1 68.1 us: local_kernel(): pl.pallas_call(functools.partial(layer_kernel, n_chips), out_shape=jax.Sh...]
    convert_element_type x2 -> x0, other arithmetic: 4.14 us -> none  [local_kernel(): return (clean.astype(bf), noisy.astype(bf))]
where the time goes in v1:
time: 102 us
  Pallas kernels  101 us (99%)
    pallas_call x1, Pallas kernels, local_kernel(): pl.pallas_call(functools.partial(layer_kernel, n_chips), out_shape=jax.Sh...  68.1 us
    pallas_call x1, Pallas kernels, local_kernel(): pl.pallas_call(place_kernel, out_shape=(jax.ShapeDtypeStruct((rows, model...  32.9 us

profile of v1, /device:TPU:0, one launch (start us, length us, event | category | flops | bytes accessed | tf_op | source)
XLA Modules:
  0.0 101.7 jit_solution(11419978981755816110)
XLA Ops:
  0.6 68.1 %shard_map.113.both = bf16[2,64,4096]{2,1,0:T(8,128)(2,1)} custom-call(bf16[64,4096]{1,0:T(8,128)(2,1)} %x_ref.1, s32[64]{0:T(128)} %flag_ref.1, bf16[4096]{0:T(1024)(128)(2,1)} %mask_ref.1, bf16[4096]{0:T(1024)(128)(2,1)} %gain_ref.1, s32[64,64]{1,0:T(8,128)} %vis_ref.1, f32[2,2048,128]{2,1,0:T(8,128)} %constant.2.clone.table_hbm, ...), custom_call_target="tpu_custom_call" | custom-call | flops 6000000000 | bytes 35651584 | tf_op jit(solution)/shard_map/pallas_call | solution.py:555
  68.8 32.9 %shard_map.114 = (bf16[64,4096]{1,0:T(8,128)(2,1)}, bf16[64,4096]{1,0:T(8,128)(2,1)}) custom-call(bf16[2,64,4096]{2,1,0:T(8,128)(2,1)} %shard_map.113.both), custom_call_target="tpu_custom_call" | custom-call | tf_op jit(solution)/shard_map/pallas_call | solution.py:620

commit v2 on v1

--- a/solution.py
+++ b/solution.py
@@ -515,16 +515,9 @@
             term_copy(copy, j).wait_send()
 
 
-def place_kernel(both, clean, noisy, sems):
-    half = clean.shape[0] // 2
-    copies = [
-        pltpu.make_async_copy(both.at[c, pl.ds(h * half, half)], out.at[pl.ds(h * half, half)], sems.at[c, h])
-        for c, out in enumerate((clean, noisy)) for h in range(2)
-    ]
-    for copy in copies:
-        copy.start()
-    for copy in copies:
-        copy.wait()
+def place_kernel(both, clean, noisy):
+    clean[...] = both[0]
+    noisy[...] = both[1]
 
 
 def rotary_table(length):
@@ -620,9 +613,8 @@
     return pl.pallas_call(
         place_kernel,
         out_shape=(jax.ShapeDtypeStruct((rows, model), bf), jax.ShapeDtypeStruct((rows, model), bf)),
-        in_specs=[hbm],
-        out_specs=(hbm, hbm),
-        scratch_shapes=[dma((2, 2))],
+        in_specs=[vmem],
+        out_specs=(vmem, vmem),
     )(both)
 
 

time: 102 us -> 71.2 us (0.70)
  Pallas kernels: 101 us -> 70.3 us
    pallas_call x1, Pallas kernels: 32.9 us -> 2.23 us  [local_kernel(): pl.pallas_call(place_kernel, out_shape=(jax.ShapeDtypeStruct((rows, model...]
where the time goes in v2:
time: 71.2 us; the launch traced here: 71 us
  Pallas kernels  70.3 us (99%)
    pallas_call x1, Pallas kernels, local_kernel(): pl.pallas_call(functools.partial(layer_kernel, n_chips), out_shape=jax.Sh...  68.1 us
    pallas_call x1, Pallas kernels, local_kernel(): pl.pallas_call(place_kernel, out_shape=(jax.ShapeDtypeStruct((rows, model...  2.23 us

profile of v2, /device:TPU:0, one launch (start us, length us, event | category | flops | bytes accessed | tf_op | source)
XLA Modules:
  0.0 71.0 jit_solution(11514946394344284593)
XLA Ops:
  0.6 68.1 %shard_map.113.both = bf16[2,64,4096]{2,1,0:T(8,128)(2,1)} custom-call(bf16[64,4096]{1,0:T(8,128)(2,1)} %x_ref.1, s32[64]{0:T(128)} %flag_ref.1, bf16[4096]{0:T(1024)(128)(2,1)} %mask_ref.1, bf16[4096]{0:T(1024)(128)(2,1)} %gain_ref.1, s32[64,64]{1,0:T(8,128)} %vis_ref.1, f32[2,2048,128]{2,1,0:T(8,128)} %constant.2.clone.table_hbm, ...), custom_call_target="tpu_custom_call" | custom-call | flops 6000000000 | bytes 35651584 | tf_op jit(solution)/shard_map/pallas_call | solution.py:548
  68.8 2.2 %shard_map.114 = (bf16[64,4096]{1,0:T(8,128)(2,1)}, bf16[64,4096]{1,0:T(8,128)(2,1)}) custom-call(bf16[2,64,4096]{2,1,0:T(8,128)(2,1)} %shard_map.113.both), custom_call_target="tpu_custom_call" | custom-call | tf_op jit(solution)/shard_map/pallas_call | solution.py:613
